TPU v7x, 512 devices: a whole 4x4x16 slice. The times are simulated.
512 devices in a mesh: ctx: 32 (over z, core), exp: 16 (over y, x).
Axes of the slice: x: 4, y: 4, z: 16, core: 2. Of those that a mesh axis runs over, the one named last changes fastest.
Arguments:
- tokens: bfloat16 [16384, 4096], P('ctx', 'exp'), may hold values from -7 to 7
- expert_ids: int32 [16384, 8], P('ctx'), may hold values from 0 to 31, all different within a row; in each aligned block of 512 rows (0 to 511, 512 to 1023, ...) at most 160 rows name the same one
- gate_weights: float32 [16384, 8], P('ctx'), may hold values from 0.1 to 1
- query_weight: bfloat16 [32, 4096, 128], P('exp'), may hold values from -2.578125 to 2.578125
- key_weight: bfloat16 [4096, 128], P('exp'), may hold values from -0.09375 to 0.09375
- value_weight: bfloat16 [4096, 128], P('exp'), may hold values from -0.09375 to 0.09375
- output_weight: bfloat16 [32, 128, 4096], P('exp'), may hold values from -0.5 to 0.5
Outputs:
- mixed_rows: bfloat16 [16384, 4096], P('ctx', 'exp')
Inputs may be any that keep to these rules, and one draw needn't show every extreme that they name: `expert_ids`: A token names 8 different head experts; among the tokens of one context shard (aligned blocks of 512 tokens) no head expert is named more than 160 times, and in every draw some head expert is named exactly 160 times in some block.
All inputs are finite; a program needn't handle non-finite values.
Results may differ from a plain program's by a relative error of at most 0.035.
Values may be sent and summed in bfloat16 or wider, within the bound.
A program may use at most 128 MiB of HBM per device.

v0:
```python
import math

import jax
import jax.numpy as jnp
from jax import lax
from jax.sharding import PartitionSpec as P


def per_device(
    tokens, expert_ids, gate_weights, query_weight, key_weight, value_weight, output_weight
):
    ctx_tokens = tokens.shape[0]
    slice_width = tokens.shape[1]
    routes = expert_ids.shape[1]
    local_experts = query_weight.shape[0]
    model_width = query_weight.shape[1]
    head_dim = query_weight.shape[2]
    owners = lax.axis_size("exp")
    experts = local_experts * owners
    capacity = min(ctx_tokens, max(2, 5 * ctx_tokens * routes // (4 * experts)))
    owned_slots = local_experts * capacity
    kv_weight = jnp.concatenate([key_weight, value_weight], axis=1)
    kv_partial = jnp.dot(tokens, kv_weight, preferred_element_type=jnp.float32)
    flat_ids = expert_ids.reshape(-1)
    one_hot = (flat_ids[:, None] == jnp.arange(experts, dtype=jnp.int32)[None, :]).astype(jnp.int32)
    earlier = jnp.cumsum(one_hot, axis=0) - one_hot
    slot_index = jnp.sum(earlier * one_hot, axis=1).reshape(ctx_tokens, routes)
    target = expert_ids * capacity + slot_index
    pair_token = jnp.broadcast_to(
        jnp.arange(ctx_tokens, dtype=jnp.int32)[:, None], (ctx_tokens, routes)
    ).reshape(-1)
    slot_token = (
        jnp.full((experts * capacity,), ctx_tokens, jnp.int32)
        .at[target.reshape(-1)]
        .set(pair_token)
    )
    padded = jnp.concatenate([tokens, jnp.zeros((1, slice_width), jnp.bfloat16)], axis=0)
    outgoing = padded[slot_token].reshape(owners, owned_slots, slice_width)
    arrived = lax.all_to_all(outgoing, "exp", split_axis=0, concat_axis=2, tiled=True)
    arranged = arrived.reshape(local_experts, capacity, model_width)
    queries = (
        jnp.einsum("acd,adh->ach", arranged, query_weight, preferred_element_type=jnp.float32)
        .astype(jnp.bfloat16)
        .reshape(owned_slots, head_dim)
    )
    own_slots = lax.dynamic_slice_in_dim(
        slot_token, lax.axis_index("exp") * owned_slots, owned_slots
    )
    positions = lax.axis_index("ctx") * ctx_tokens + jnp.where(own_slots < ctx_tokens, own_slots, 0)
    score_scale = 1.0 / math.sqrt(head_dim)
    shares = lax.psum_scatter(
        kv_partial.astype(jnp.bfloat16), "exp", scatter_dimension=0, tiled=True
    )
    portion = lax.all_gather(shares, ("ctx", "exp"), axis=0, tiled=True)
    key_part = portion[:, :head_dim]
    value_part = portion[:, head_dim:]
    length = portion.shape[0]
    running_max = jnp.full((owned_slots,), -1e30, jnp.float32)
    scores = (
        jnp.einsum("qh,kh->qk", queries, key_part, preferred_element_type=jnp.float32) * score_scale
    )
    visible = jnp.arange(length, dtype=jnp.int32)[None, :] <= positions[:, None]
    masked = jnp.where(visible, scores, -1e30)
    new_max = jnp.maximum(running_max, jnp.max(masked, axis=1))
    weights = jnp.where(visible, jnp.exp(masked - new_max[:, None]), 0.0)
    weight_sum = jnp.sum(weights, axis=1)
    accumulated = jnp.dot(
        weights.astype(jnp.bfloat16), value_part, preferred_element_type=jnp.float32
    )
    result = (new_max, weight_sum, accumulated)
    weight_sum = result[1]
    accumulated = result[2]
    head_rows = (
        (accumulated / weight_sum[:, None])
        .astype(jnp.bfloat16)
        .reshape(local_experts, capacity, head_dim)
    )
    produced = jnp.einsum(
        "ach,ahn->acn", head_rows, output_weight, preferred_element_type=jnp.float32
    ).astype(jnp.bfloat16)
    returned = lax.all_to_all(
        produced.reshape(1, owned_slots, model_width),
        "exp",
        split_axis=2,
        concat_axis=0,
        tiled=True,
    )
    flat_out = returned.reshape(experts * capacity, slice_width)
    picked = flat_out[target]
    mixed_rows = jnp.sum(gate_weights[:, :, None] * picked.astype(jnp.float32), axis=1)
    return mixed_rows.astype(jnp.bfloat16)


def solution(mesh):
    in_specs = (
        P("ctx", "exp"),
        P("ctx", None),
        P("ctx", None),
        P("exp", None, None),
        P("exp", None),
        P("exp", None),
        P("exp", None, None),
    )
    out_specs = P("ctx", "exp")
    return jax.shard_map(
        per_device, mesh=mesh, in_specs=in_specs, out_specs=out_specs, check_vma=False
    )
```

profile of v0, /device:TPU:1, one launch (start us, length us, event | category | flops | bytes accessed | tf_op | source)
XLA Modules:
  0.0 545.1 jit_solution(3647507186013489836)
XLA Ops:
  6.5 0.0 copy-start
  6.5 0.0 copy-start.2
  6.5 0.0 copy-start.3
  6.5 0.0 reduce-scatter.4.cloned.1.call-start
  6.5 1.4 fusion.8
  8.0 0.8 copy.49
  8.8 0.0 reduce-scatter.4.cloned.1.call-update
  8.9 0.0 all-gather.2.cloned.1.call-start
  8.9 93.5 %reduce-scatter.4.cloned.1.call-done = bf16[32,256]{1,0:T(8,128)(2,1)} async-done(((bf16[512,256]{1,0:T(8,128)(2,1)}), bf16[32,256]{1,0:T(8,128)(2,1)}) %reduce-scatter.4.cloned.1.call-update) | async-done | bytes 16400 | tf_op jit(solution)/shard_map/reduce_scatter | solution.py:51
  102.4 0.0 all-gather.2.cloned.1.call-update
  102.5 0.8 copy.38
  103.3 0.1 eq.29
  103.5 0.1 eq.25
  103.6 0.1 fusion.22
  103.7 9.2 %reduce-window.6 = s32[32,32,128]{2,1,0:T(8,128)S(1)} reduce-window(s32[32,32,128]{2,1,0:T(8,128)S(1)} %fusion.22, s32[]{:T(128)} %constant.18.clone.1), window={size=1x1x128 pad=0_0x0_0x127_0}, to_apply=%region_0.0 | reduce-window | flops 16646144 | bytes 1048580 | tf_op jit(solution)/shard_map/reduce-window
  112.9 0.8 slice_reduce_fusion
  113.7 0.2 reduce-window.9
  113.9 0.2 broadcast_add_fusion
  114.1 0.4 fusion.21
  114.5 0.2 reshape.81
  114.6 0.1 copy.40
  114.7 0.0 copy-done.3
  114.8 0.1 copy.41
  114.9 0.2 reshape.82
  115.1 0.1 reshape.110
  115.3 0.0 copy-done.2
  115.3 15.5 %scatter_custom_fusion = s32[5120]{0:T(1024)S(1)} fusion(s32[4096]{0:T(1024)S(1)} %bitcast.56, s32[4096]{0:T(1024)S(1)} %reshape.110, s32[]{:T(128)} %constant.16.clone.1), kind=kCustom, calls=%fused_computation.37 | custom fusion | bytes 20484 | tf_op jit(solution)/shard_map/scatter | solution.py:35
  130.9 21.0 %gather_fusion = bf16[5120,256]{1,0:T(8,128)(2,1)} fusion(bf16[513,256]{1,0:T(8,128)(2,1)S(1)} %concatenate.6, s32[5120]{0:T(1024)S(1)} %fusion.26), kind=kCustom, calls=%fused_computation | custom fusion | bytes 5263360 | tf_op jit(solution)/shard_map/gather | solution.py:38
  151.9 4.6 all-to-all-start
  156.5 0.1 fusion.29
  156.6 32.0 %all-to-all-done = bf16[16,320,256]{2,1,0:T(8,128)(2,1)} async-done(((bf16[16,320,256]{2,1,0:T(8,128)(2,1)}), bf16[16,320,256]{2,1,0:T(8,128)(2,1)}, u32[]{:S(2)}, u32[]{:S(2)}) %all-to-all-start) | async-done | bytes 2621472 | tf_op jit(solution)/shard_map/all_to_all | solution.py:39
  188.6 4.7 copy.42
  193.3 5.3 reshape.85
  198.6 3.3 convolution_convert_fusion.2
  201.9 119.2 %all-gather.2.cloned.1.call-done = bf16[16384,256]{1,0:T(8,128)(2,1)} async-done(((bf16[32,256]{1,0:T(8,128)(2,1)}), bf16[16384,256]{1,0:T(8,128)(2,1)}) %all-gather.2.cloned.1.call-update) | async-done | bytes 8388624 | tf_op jit(solution)/shard_map/all_gather | solution.py:54
  321.1 5.8 %fusion.32 = (f32[320]{0:T(512)S(1)}, f32[320,16384]{1,0:T(8,128)S(1)}) fusion(bf16[320,128]{1,0:T(8,128)(2,1)S(1)} %bitcast.53, bf16[16384,256]{1,0:T(8,128)(2,1)} %all-gather.2.cloned.1.call-done, s32[320]{0:T(512)S(1)} %fusion.29), kind=kOutput, calls=%fused_computation.45 | convolution fusion | flops 1363148544 | bytes 25250304 | tf_op jit(solution)/shard_map/qh,kh->qk/dot_general | solution.py:60
  326.9 0.0 copy-start.1
  326.9 7.0 %copy-done.1 = f32[320,16384]{1,0:T(8,128)} copy-done((f32[320,16384]{1,0:T(8,128)}, f32[320,16384]{1,0:T(8,128)S(1)}, u32[]{:S(2)}) %copy-start.1) | copy-done | bytes 20971544
  333.8 5.7 %fusion.1 = f32[320]{0:T(512)S(1)} fusion(f32[320,16384]{1,0:T(8,128)S(1)} %get-tuple-element.8, f32[320]{0:T(512)S(1)} %broadcast_maximum_fusion, s32[320]{0:T(512)S(1)} %fusion.29), kind=kLoop, calls=%fused_computation.7 | loop fusion | flops 20971200 | bytes 20975360 | tf_op jit(solution)/shard_map/reduce_sum | solution.py:66
  339.5 10.6 %fusion.14 = bf16[320,128]{1,0:T(8,128)(2,1)S(1)} fusion(bf16[16384,256]{1,0:T(8,128)(2,1)} %all-gather.2.cloned.1.call-done, f32[320,16384]{1,0:T(8,128)} %copy-done.1, f32[320]{0:T(512)S(1)} %broadcast_maximum_fusion, s32[320]{0:T(512)S(1)} %fusion.29, f32[320]{0:T(512)S(1)} %fusion.1), kind=kOutput, calls=%fused_computation.19 | convolution fusion | flops 1363230720 | bytes 25251584 | tf_op jit(solution)/shard_map/dot_general | solution.py:67
  350.1 0.0 copy-done
  350.1 2.4 convolution_convert_fusion
  352.5 14.3 %copy.44 = bf16[1,320,4096]{1,0,2:T(2,128)(2,1)} copy(bf16[1,320,4096]{2,1,0:T(8,128)(2,1)} %bitcast.50) | data formatting | bytes 5242880 | tf_op jit(solution)/shard_map/reshape | solution.py:82
  366.8 0.5 broadcast.50
  367.4 69.0 %reduce.2 = bf16[4096,320]{1,0:T(8,128)(2,1)} reduce(bf16[4096,1,320]{2,1,0:T(2,128)(2,1)} %bitcast.46, bf16[]{:T(256)} %broadcast.50), dimensions={1}, to_apply=%bitcast.36.reduce_sub_computation | reduce | bytes 5242882
  436.3 7.6 %reshape.124 = bf16[16,2,40960]{2,1,0:T(2,128)(2,1)} reshape(bf16[4096,320]{1,0:T(8,128)(2,1)} %reduce.2) | data formatting | bytes 5242880
  443.9 0.0 copy-start.4
  443.9 5.2 all-to-all-start.1
  449.1 0.1 copy.47
  449.3 0.2 reshape.100
  449.4 0.0 copy-done.4
  449.4 0.1 copy.37
  449.6 39.3 %all-to-all-done.1 = bf16[16,2,40960]{2,1,0:T(2,128)(2,1)} async-done(((bf16[16,2,40960]{2,1,0:T(2,128)(2,1)}), bf16[16,2,40960]{2,1,0:T(2,128)(2,1)}, u32[]{:S(2)}, u32[]{:S(2)}) %all-to-all-start.1) | async-done | bytes 2621472 | tf_op jit(solution)/shard_map/all_to_all | solution.py:81
  488.9 12.6 %reshape.125 = bf16[4096,1,320]{2,1,0:T(2,128)(2,1)} reshape(bf16[16,2,40960]{2,1,0:T(2,128)(2,1)} %all-to-all-done.1) | data formatting | bytes 5242880
  501.5 5.0 copy.51
  506.5 4.9 copy.48
  511.4 4.2 copy.46
  515.6 17.9 %gather_fusion.1 = bf16[4096,256]{1,0:T(8,128)(2,1)} fusion(bf16[5120,256]{1,0:T(8,128)(2,1)} %bitcast.45, s32[4096]{0:T(1024)S(1)} %broadcast_clamp_fusion), kind=kCustom, calls=%fused_computation.1 | custom fusion | bytes 4210688 | tf_op jit(solution)/shard_map/gather | solution.py:89
  533.5 4.8 fusion.7
  (7 shorter events, 0.1 us)
Async XLA Ops:
  6.5 343.6 %copy-start = (bf16[2,128,4096]{2,1,0:T(8,128)(2,1)S(1)}, bf16[2,128,4096]{2,1,0:T(8,128)(2,1)}, u32[]{:S(2)}) copy-start(bf16[2,128,4096]{2,1,0:T(8,128)(2,1)} %param.13) | copy-start | bytes 6291460
  6.5 108.7 %copy-start.2 = (bf16[512,256]{1,0:T(8,128)(2,1)S(1)}, bf16[512,256]{1,0:T(8,128)(2,1)}, u32[]{:S(2)}) copy-start(bf16[512,256]{1,0:T(8,128)(2,1)} %param.7) | copy-start | bytes 786436
  6.5 108.2 %copy-start.3 = (s32[512,8]{0,1:T(8,128)S(1)}, s32[512,8]{0,1:T(8,128)}, u32[]{:S(2)}) copy-start(s32[512,8]{0,1:T(8,128)} %param.8) | copy-start | bytes 49156
  6.5 95.9 %reduce-scatter.4.cloned.1.call-start = ((), (), s32[]{:S(2)}) async-start(), calls=%async_computation.4 | async-start | bytes 278528 | tf_op jit(solution)/shard_map/reduce_scatter | solution.py:51
  8.9 312.2 %all-gather.2.cloned.1.call-start = ((), (), s32[]{:S(2)}) async-start(), calls=%async_computation.3 | async-start | bytes 8404992 | tf_op jit(solution)/shard_map/all_gather | solution.py:54
  151.9 36.7 %all-to-all-start = ((bf16[16,320,256]{2,1,0:T(8,128)(2,1)}), bf16[16,320,256]{2,1,0:T(8,128)(2,1)}, u32[]{:S(2)}, u32[]{:S(2)}) async-start(bf16[16,320,256]{2,1,0:T(8,128)(2,1)} %bitcast.51), calls=%async_computation | async-start | bytes 5242880 | tf_op jit(solution)/shard_map/all_to_all | solution.py:39
  326.9 7.0 %copy-start.1 = (f32[320,16384]{1,0:T(8,128)}, f32[320,16384]{1,0:T(8,128)S(1)}, u32[]{:S(2)}) copy-start(f32[320,16384]{1,0:T(8,128)S(1)} %get-tuple-element.8) | copy-start | bytes 62914564
  443.9 5.5 %copy-start.4 = (f32[512,8]{0,1:T(8,128)S(1)}, f32[512,8]{0,1:T(8,128)}, u32[]{:S(2)}) copy-start(f32[512,8]{0,1:T(8,128)} %param.9) | copy-start | bytes 49156
  443.9 45.0 %all-to-all-start.1 = ((bf16[16,2,40960]{2,1,0:T(2,128)(2,1)}), bf16[16,2,40960]{2,1,0:T(2,128)(2,1)}, u32[]{:S(2)}, u32[]{:S(2)}) async-start(bf16[16,2,40960]{2,1,0:T(2,128)(2,1)} %reshape.124), calls=%async_computation.1 | async-start | bytes 5242880 | tf_op jit(solution)/shard_map/all_to_all | solution.py:81
Sparse Core Ops, SparseCore 0:
  11.4 90.9 reduce-scatter.3
  107.9 213.1 all-gather.1
where the time goes:
time: 547 us; the launch traced here: 545 us
  waiting for transfers between devices  284 us (52%)
  local copies, waits for them, and re-layouts  124 us (23%)
  other arithmetic  89.6 us (16%)
  matrix products  23.4 us (4%)
  between operations  13.6 us (2%)
  starting transfers between devices  9.92 us (2%)
    all_gather x1, waiting for transfers between devices, per_device(): portion = lax.all_gather(shares, ('ctx', 'exp'), axis=0, tiled=True)  119 us
    reduce_scatter x1, waiting for transfers between devices, per_device(): lax.psum_scatter(kv_partial.astype(jnp.bfloat16), 'exp', scatter_dimensio...  93.5 us
    unnamed x1, other arithmetic  69 us
    all_to_all x1, waiting for transfers between devices, per_device(): lax.all_to_all(produced.reshape(1, owned_slots, model_width), 'exp', spli...  39.3 us
    unnamed x17, local copies, waits for them, and re-layouts  34.5 us
    all_to_all x1, waiting for transfers between devices, per_device(): lax.all_to_all(outgoing, 'exp', split_axis=0, concat_axis=2, tiled=True)  32 us
    gather x1, local copies, waits for them, and re-layouts, per_device(): outgoing = padded[slot_token].reshape(owners, owned_slots, slice_width)  21 us
    gather x1, local copies, waits for them, and re-layouts, per_device(): picked = flat_out[target]  17.9 us
  transfers between devices with their start and end apart: 4, of which 4 were waited for; matrix products, arithmetic and copies ran while one was open for 12% of the time, Pallas kernels for 0%

commit v1 on v0

v1 whole, which is shorter than its diff:
```python
import functools
import math

import jax
import jax.numpy as jnp
from jax import lax
from jax.experimental import pallas as pl
from jax.experimental.pallas import tpu as pltpu
from jax.sharding import PartitionSpec as P

MESH = pl.DeviceIdType.MESH
RING = 4
PEERS = RING * RING
LANES = 256
LOWEST = -1e30


def nt_dot(a, b):
    return lax.dot_general(a, b, (((1,), (1,)), ((), ())), preferred_element_type=jnp.float32)


def tn_dot(a, b):
    return lax.dot_general(a, b, (((0,), (0,)), ((), ())), preferred_element_type=jnp.float32)


def dot(a, b):
    return jnp.dot(a, b, preferred_element_type=jnp.float32)


def drain(ref, sem):
    pltpu.make_async_copy(ref, ref, sem).wait()


class PlaneGather:
    def __init__(self, buf, rows, send_sem, recv_sem, place):
        self.buf, self.rows = buf, rows
        self.send_sem, self.recv_sem, self.place = send_sem, recv_sem, place
        self.started = []

    def slot(self, half, first, second):
        return second * RING + first if half == 0 else first * RING + second

    def message(self, half, phase, other, where):
        rows = self.rows // 2
        index = {3: 0, 1: 1, "2a": 2, "2b": 3}[where]
        number = half * 20 + (index if phase == 0 else 4 + other * 4 + index)
        begin = half * rows
        if where in ("2a", "2b"):
            rows = rows // 2
            if where == "2b":
                begin += rows
        step = 1 if where in (3, "2a") else 3
        source = {3: 0, 1: 0, "2a": 3, "2b": 1}[where]
        target = int(str(where)[0])
        if phase == 0:
            src, dst = self.slot(half, source, 0), self.slot(half, target, 0)
        else:
            src, dst = self.slot(half, other, source), self.slot(half, other, target)
        along_x = (half == 0) == (phase == 0)
        device = self.place(0, step) if along_x else self.place(step, 0)
        return pltpu.make_async_remote_copy(
            src_ref=self.buf.at[src, pl.ds(begin, rows)],
            dst_ref=self.buf.at[dst, pl.ds(begin, rows)],
            send_sem=self.send_sem.at[number],
            recv_sem=self.recv_sem.at[number],
            device_id=device,
            device_id_type=MESH,
        )

    def start(self, *key):
        copy = self.message(*key)
        copy.start()
        self.started.append(copy)

    def wait(self, *key):
        self.message(*key).wait_recv()

    def finish(self):
        for copy in self.started:
            copy.wait_send()

    def run(self, arrived, beside=lambda stage: None):
        for half in range(2):
            self.start(half, 0, 0, 3)
            self.start(half, 0, 0, 1)
        for half in range(2):
            self.start(half, 1, 0, 3)
            self.start(half, 1, 0, 1)
        beside(0)
        arrived(0, 0)
        arrived(1, 0)
        for half in range(2):
            for where, onward in ((3, "2a"), (1, "2b")):
                self.wait(half, 0, 0, where)
                self.start(half, 0, 0, onward)
                self.start(half, 1, where, 3)
                self.start(half, 1, where, 1)
        for half in range(2):
            for where in (3, 1):
                arrived(half, self.slot(half, where, 0))
        beside(1)
        for half in range(2):
            for where, onward in ((3, "2a"), (1, "2b")):
                self.wait(half, 1, 0, where)
                self.start(half, 1, 0, onward)
        for half in range(2):
            self.wait(half, 0, 0, "2a")
            self.wait(half, 0, 0, "2b")
            self.start(half, 1, 2, 3)
            self.start(half, 1, 2, 1)
        for half in range(2):
            for where in (3, 1):
                arrived(half, self.slot(half, 0, where))
            arrived(half, self.slot(half, 2, 0))
        beside(2)
        for other in (3, 1):
            for half in range(2):
                for where, onward in ((3, "2a"), (1, "2b")):
                    self.wait(half, 1, other, where)
                    self.start(half, 1, other, onward)
                    arrived(half, self.slot(half, other, where))
        beside(3)
        for half in range(2):
            self.wait(half, 1, 0, "2a")
            self.wait(half, 1, 0, "2b")
            arrived(half, self.slot(half, 0, 2))
        for half in range(2):
            for where, onward in ((3, "2a"), (1, "2b")):
                self.wait(half, 1, 2, where)
                self.start(half, 1, 2, onward)
                arrived(half, self.slot(half, 2, where))
        beside(4)
        for other in (3, 1, 2):
            for half in range(2):
                self.wait(half, 1, other, "2a")
                self.wait(half, 1, other, "2b")
                arrived(half, self.slot(half, other, 2))
        beside(5)


def layer(
    capacity,
    tokens,
    expert_ids,
    gates,
    query_weight,
    key_weight,
    value_weight,
    output_weight,
    out,
    tok,
    qw,
    kv_part,
    kv_in,
    kv,
    q_sum,
    q_all,
    slot_of,
    gate_of,
    spread,
    where_row,
    wout,
    top_score,
    num,
    part_out,
    part_lse,
    heads,
    produced,
    total,
    tok_send,
    tok_recv,
    head_send,
    head_recv,
    peer_send,
    peer_recv,
    local,
):
    ctx, exp = lax.axis_index("ctx"), lax.axis_index("exp")
    y, x = exp // RING, exp % RING
    z, core = ctx // 2, ctx % 2
    depth = kv.shape[0]
    t, f = tokens.shape
    routes = expert_ids.shape[1]
    mine = query_weight.shape[0]
    hd = query_weight.shape[2]
    share = t // PEERS
    owned = mine * capacity

    def place(dy, dx):
        return (ctx, ((y + dy) % RING) * RING + (x + dx) % RING)

    sibling = (ctx + 1 - 2 * core, exp)

    def send(src, dst, send_sem, recv_sem, device):
        return pltpu.make_async_remote_copy(
            src_ref=src, dst_ref=dst, send_sem=send_sem, recv_sem=recv_sem, device_id=device, device_id_type=MESH
        )

    barrier = pltpu.get_barrier_semaphore()

    @pl.loop(1, PEERS)
    def _(i):
        pl.semaphore_signal(barrier, inc=1, device_id=(ctx, (exp + i) % PEERS), device_id_type=MESH)

    @pl.loop(1, depth)
    def _(i):
        pl.semaphore_signal(barrier, inc=1, device_id=(((z + i) % depth) * 2 + core, exp), device_id_type=MESH)

    pl.semaphore_signal(barrier, inc=1, device_id=sibling, device_id_type=MESH)

    load_qw = pltpu.make_async_copy(query_weight, qw, local.at[0])
    load_qw.start()
    own_width = pl.ds(pl.multiple_of(exp * f, f), f)
    load_wout = pltpu.make_async_copy(output_weight.at[core, :, own_width], wout.at[0, core], local.at[1])
    load_wout.start()

    tok[0] = tokens[...]
    kv_part[:, :hd] = dot(tokens[...], key_weight[...]).astype(jnp.bfloat16)
    kv_part[:, hd:] = dot(tokens[...], value_weight[...]).astype(jnp.bfloat16)

    column = lax.broadcasted_iota(jnp.int32, (1, 128), 1)
    at = column // mine
    expert = ((((y + at // RING) % RING) * RING) + (x + at % RING) % RING) * mine + column % mine
    routed = jnp.zeros((t, 128), jnp.float32)
    gate_sum = jnp.zeros((t, 128), jnp.float32)
    for r in range(routes):
        hit = expert_ids[:, r : r + 1] == expert
        routed = jnp.where(hit, 1.0, routed)
        gate_sum = jnp.where(hit, gates[:, r : r + 1], gate_sum)
    gate_of[...] = gate_sum
    earlier = jnp.where(
        lax.broadcasted_iota(jnp.int32, (t, t), 1) < lax.broadcasted_iota(jnp.int32, (t, t), 0), 1.0, 0.0
    ).astype(jnp.bfloat16)
    slot_of[...] = jnp.where(routed > 0.5, dot(earlier, routed.astype(jnp.bfloat16)), -1.0)

    pl.semaphore_wait(barrier, PEERS - 1 + depth - 1 + 1)

    @pl.loop(1, PEERS)
    def _(i):
        j = (exp + i) % PEERS
        send(
            kv_part.at[pl.ds(pl.multiple_of(j * share, share), share)],
            kv_in.at[i],
            peer_send.at[0],
            peer_recv.at[0],
            (ctx, j),
        ).start()

    gather = PlaneGather(tok, t, tok_send, tok_recv, place)
    q_sum[...] = jnp.zeros_like(q_sum)

    def add_queries(half, slot):
        rows = pl.ds(half * (t // 2), t // 2)
        owner = ((y + slot // RING) % RING) * RING + (x + slot % RING) % RING
        features = pl.ds(pl.multiple_of(owner * f, f), f)
        piece = tok[slot, rows]
        for a in range(mine):
            q_sum[a, rows] += dot(piece, qw[a, features])

    x1, x2, x3 = (x + 1) % RING, (x + 2) % RING, (x + 3) % RING
    half_z = depth // 2
    lower, upper = pl.ds(0, half_z), pl.ds(half_z, half_z)
    to_right = send(kv.at[:, core, x], kv.at[:, core, x], peer_send.at[2], peer_recv.at[2], place(0, 1))
    to_left = send(kv.at[:, core, x], kv.at[:, core, x], peer_send.at[3], peer_recv.at[3], place(0, 3))
    on_right = send(kv.at[lower, core, x3], kv.at[lower, core, x3], peer_send.at[4], peer_recv.at[4], place(0, 1))
    on_left = send(kv.at[upper, core, x1], kv.at[upper, core, x1], peer_send.at[5], peer_recv.at[5], place(0, 3))

    def got(piece, number, device):
        return send(piece, piece, peer_send.at[number], peer_recv.at[number], device)

    from_left = got(kv.at[:, core, x3], 2, place(0, 1))
    from_right = got(kv.at[:, core, x1], 3, place(0, 3))
    far_lower = got(kv.at[lower, core, x2], 4, place(0, 1))
    far_upper = got(kv.at[upper, core, x2], 5, place(0, 3))
    across = [
        send(kv.at[:, core, xx], kv.at[:, core, xx], peer_send.at[6 + n], peer_recv.at[6 + n], sibling)
        for n, xx in enumerate((x, x3, x1, x2))
    ]
    other_core = 1 - core
    across_in = [
        got(kv.at[:, other_core, xx], 6 + n, sibling) for n, xx in enumerate((x, x3, x1, x2))
    ]

    def one_hot(n, values):
        lane = lax.broadcasted_iota(jnp.int32, (t, 128), 1)
        pick = lane == n
        slot = jnp.sum(jnp.where(pick, slot_of[...], 0.0), axis=1, keepdims=True)
        if values is None:
            value = jnp.ones((t, 1), jnp.float32)
        else:
            value = jnp.sum(jnp.where(pick, values[...], 0.0), axis=1, keepdims=True)
        lanes = lax.broadcasted_iota(jnp.int32, (t, LANES), 1).astype(jnp.float32)
        return jnp.where(slot == lanes, value, 0.0).astype(jnp.bfloat16)

    def beside(stage):
        if stage == 0:
            drain(kv_in.at[pl.ds(1, PEERS - 1)], peer_recv.at[0])
            summed = kv_part[pl.ds(pl.multiple_of(exp * share, share), share)].astype(jnp.float32)
            for i in range(1, PEERS):
                summed += kv_in[i].astype(jnp.float32)
            kv[z, core, x] = summed.astype(jnp.bfloat16)

            @pl.loop(1, depth)
            def _(i):
                zz = (z + i) % depth
                send(
                    kv.at[z, core, x], kv.at[z, core, x], peer_send.at[1], peer_recv.at[1], (zz * 2 + core, exp)
                ).start()

            load_qw.wait()
        elif stage == 1:

            @pl.loop(0, PEERS * mine)
            def _(n):
                spread[n] = one_hot(n, gate_of)

        elif stage == 2:
            position = lax.broadcasted_iota(jnp.int32, (t, 128), 0)
            high = (position // 16).astype(jnp.float32).astype(jnp.bfloat16)
            low = (position % 16).astype(jnp.float32).astype(jnp.bfloat16)
            place_of = jnp.concatenate([high, low], axis=1)

            @pl.loop(0, RING * mine)
            def _(n):
                at = tn_dot(one_hot((n // mine) * (RING * mine) + n % mine, None), place_of)
                where_row[n] = 16.0 * at[:capacity, :128] + at[:capacity, 128:]

        elif stage == 3:
            drain(kv.at[pl.ds(1, depth - 1), core, x], peer_recv.at[1])
            to_right.start()
            to_left.start()
            across[0].start()
        elif stage == 4:
            from_left.wait_recv()
            on_right.start()
            across[1].start()
            from_right.wait_recv()
            on_left.start()
            across[2].start()

    gather.run(add_queries, beside)

    for a in range(mine):
        rows = q_sum[a].astype(jnp.bfloat16)
        q_all[0, pl.ds(a * capacity, capacity)] = tn_dot(one_hot(a, None), rows)[:capacity].astype(jnp.bfloat16)
    q_moves = [
        send(q_all.at[0], q_all.at[RING - dy], peer_send.at[10 + dy], peer_recv.at[10 + dy], place(dy, 0))
        for dy in range(1, RING)
    ]
    for move in q_moves:
        move.start()

    far_lower.wait_recv()
    far_upper.wait_recv()
    across[3].start()

    @pl.loop(1, PEERS)
    def _(i):
        dy, dx = i // RING, i % RING
        j = ((y + dy) % RING) * RING + (x + dx) % RING
        back = ((RING - dy) % RING) * RING + (RING - dx) % RING
        send(
            output_weight.at[core, :, pl.ds(pl.multiple_of(j * f, f), f)],
            wout.at[back, core],
            peer_send.at[16],
            peer_recv.at[16],
            (ctx, j),
        ).start()

    for copy in across_in:
        copy.wait_recv()

    factor = math.log2(math.e) / math.sqrt(hd)
    groups = ctx // 4
    block = 4 * RING * share

    def attend(dy):
        top_score[...] = jnp.full_like(top_score, LOWEST)
        num[...] = jnp.zeros_like(num)

        def step(g, masked):
            keys = kv[pl.ds(2 * g, 2)].reshape(block, 2 * hd)
            values = jnp.concatenate([keys[:, hd:], jnp.ones((block, hd), jnp.bfloat16)], axis=1)
            keys = keys[:, :hd]
            for a in range(mine):
                rows = pl.ds(a * capacity, capacity)
                scores = nt_dot(q_all[dy, rows], keys)
                if masked:
                    index = lax.broadcasted_iota(jnp.int32, (1, block), 1)
                    span = RING * share
                    at = (4 * g + index // span - ctx) * t + y * span + index % span
                    scores = jnp.where(
                        at.astype(jnp.float32) <= where_row[dy * mine + a][:, 0:1], scores, LOWEST
                    )
                before = top_score[rows, 0:1]
                now = jnp.maximum(before, jnp.max(scores, axis=1, keepdims=True))
                weights = jnp.exp2((scores - now) * factor).astype(jnp.bfloat16)
                num[rows] = num[rows] * jnp.exp2((before - now) * factor) + dot(weights, values)
                top_score[rows] = jnp.broadcast_to(now, (capacity, 128))

        @pl.loop(0, groups)
        def _(g):
            step(g, False)

        step(groups, True)
        for a in range(mine):
            rows = pl.ds(a * capacity, capacity)
            norm = num[rows, hd:]
            part_out[dy, rows] = (num[rows, :hd] / norm).astype(jnp.bfloat16)
            lse = top_score[rows, 0:1] * factor + jnp.log2(norm[:, 0:1])
            part_lse[dy, pl.ds(a * 8, 8)] = to_row(lse)

    def diagonal():
        return lax.broadcasted_iota(jnp.int32, (capacity, LANES), 0) == lax.broadcasted_iota(
            jnp.int32, (capacity, LANES), 1
        )

    def to_row(values):
        row = jnp.sum(jnp.where(diagonal(), values, 0.0), axis=0, keepdims=True)
        return jnp.broadcast_to(row, (8, LANES))

    def to_column(row):
        return jnp.sum(jnp.where(diagonal(), row, 0.0), axis=1, keepdims=True)

    moves = []
    for dy in (2, 1, 3, 0):
        if dy:
            q_moves[RING - dy - 1].wait_recv()
        attend(dy)
        if dy:
            moves.append(
                send(part_out.at[dy], part_out.at[8 - dy], peer_send.at[17 + dy], peer_recv.at[17 + dy], place(dy, 0))
            )
            moves.append(
                send(part_lse.at[dy], part_lse.at[8 - dy], peer_send.at[21 + dy], peer_recv.at[21 + dy], place(dy, 0))
            )
            moves[-2].start()
            moves[-1].start()

    load_wout.wait()
    drain(wout.at[pl.ds(1, PEERS - 1), core], peer_recv.at[16])
    weights_across = send(wout.at[:, core], wout.at[:, core], peer_send.at[17], peer_recv.at[17], sibling)
    weights_across.start()
    produced[...] = jnp.zeros_like(produced)
    total[...] = jnp.zeros_like(total)

    for move in moves:
        move.wait_recv()
    for a in range(mine):
        rows = pl.ds(a * capacity, capacity)
        slots = (0, 5, 6, 7)
        lses = [to_column(part_lse[s, pl.ds(a * 8, 1)]) for s in slots]
        top = functools.reduce(jnp.maximum, lses)
        shares = [jnp.exp2(lse - top) for lse in lses]
        norm = functools.reduce(jnp.add, shares)
        rows_sum = functools.reduce(
            jnp.add, [w * part_out[s, rows].astype(jnp.float32) for w, s in zip(shares, slots)]
        )
        heads[0, rows] = (rows_sum / norm).astype(jnp.bfloat16)

    got(wout.at[:, other_core], 17, sibling).wait_recv()

    def add_output(half, slot):
        n = slot * mine + half
        made = dot(heads[slot, pl.ds(half * capacity, capacity)], wout[slot, half])
        produced[half, pl.ds(0, capacity)] = made.astype(jnp.bfloat16)
        total[...] += dot(spread[n], produced[half])

    head_gather = PlaneGather(heads, owned, head_send, head_recv, place)
    head_gather.run(add_output)
    out[...] = total[...].astype(jnp.bfloat16)

    gather.finish()
    head_gather.finish()
    drain(kv_in.at[pl.ds(1, PEERS - 1)], peer_send.at[0])
    drain(kv.at[pl.ds(1, depth - 1), core, x], peer_send.at[1])
    drain(wout.at[pl.ds(1, PEERS - 1), core], peer_send.at[16])
    for copy in (to_right, to_left, on_right, on_left, weights_across, *across, *q_moves, *moves):
        copy.wait_send()


def per_device(depth, tokens, expert_ids, gates, query_weight, key_weight, value_weight, output_weight):
    t, f = tokens.shape
    routes = expert_ids.shape[1]
    mine, model, hd = query_weight.shape
    experts = mine * PEERS
    capacity = min(t, max(2, 5 * t * routes // (4 * experts)))
    owned = mine * capacity
    share = t // PEERS
    bf16, f32 = jnp.bfloat16, jnp.float32
    vmem, anywhere = pl.BlockSpec(memory_space=pltpu.VMEM), pl.BlockSpec(memory_space=pl.ANY)
    return pl.pallas_call(
        functools.partial(layer, capacity),
        out_shape=jax.ShapeDtypeStruct((t, f), bf16),
        in_specs=[vmem, vmem, vmem, anywhere, vmem, vmem, anywhere],
        out_specs=vmem,
        scratch_shapes=[
            pltpu.VMEM((PEERS, t, f), bf16),
            pltpu.VMEM((mine, model, hd), bf16),
            pltpu.VMEM((t, 2 * hd), bf16),
            pltpu.VMEM((PEERS, share, 2 * hd), bf16),
            pltpu.VMEM((depth, 2, RING, share, 2 * hd), bf16),
            pltpu.VMEM((mine, t, hd), f32),
            pltpu.VMEM((RING, owned, hd), bf16),
            pltpu.VMEM((t, 128), f32),
            pltpu.VMEM((t, 128), f32),
            pltpu.VMEM((experts, t, LANES), bf16),
            pltpu.VMEM((RING * mine, capacity, 128), f32),
            pltpu.VMEM((PEERS, mine, hd, f), bf16),
            pltpu.VMEM((owned, 128), f32),
            pltpu.VMEM((owned, 2 * hd), f32),
            pltpu.VMEM((2 * RING, owned, hd), bf16),
            pltpu.VMEM((2 * RING, 8 * mine, LANES), f32),
            pltpu.VMEM((PEERS, owned, hd), bf16),
            pltpu.VMEM((mine, LANES, f), bf16),
            pltpu.VMEM((t, f), f32),
            pltpu.SemaphoreType.DMA((40,)),
            pltpu.SemaphoreType.DMA((40,)),
            pltpu.SemaphoreType.DMA((40,)),
            pltpu.SemaphoreType.DMA((40,)),
            pltpu.SemaphoreType.DMA((25,)),
            pltpu.SemaphoreType.DMA((25,)),
            pltpu.SemaphoreType.DMA((2,)),
        ],
        compiler_params=pltpu.CompilerParams(
            collective_id=0, has_side_effects=True, vmem_limit_bytes=56 * 1024 * 1024
        ),
    )(tokens, expert_ids, gates, query_weight, key_weight, value_weight, output_weight)


def solution(mesh):
    in_specs = (
        P("ctx", "exp"),
        P("ctx", None),
        P("ctx", None),
        P("exp", None, None),
        P("exp", None),
        P("exp", None),
        P("exp", None, None),
    )
    out_specs = P("ctx", "exp")
    return jax.shard_map(
        functools.partial(per_device, mesh.shape["ctx"] // 2),
        mesh=mesh,
        in_specs=in_specs,
        out_specs=out_specs,
        check_vma=False,
    )
```

time: 547 us -> 108 us (0.20)
  the two profiles are of different devices: /device:TPU:1 before, /device:TPU:489 now
where the time goes in v1:
time: 108 us
  Pallas kernels  103 us (95%)
  local copies, waits for them, and re-layouts  4.76 us (4%)
    pallas_call x1, Pallas kernels, per_device(): pl.pallas_call(functools.partial(layer, capacity), out_shape=jax.ShapeDty...  103 us
    unnamed x3, local copies, waits for them, and re-layouts  4.76 us

profile of v1, /device:TPU:489, one launch (start us, length us, event | category | flops | bytes accessed | tf_op | source)
XLA Modules:
  0.0 107.7 jit_solution(13355312014558031293)
XLA Ops:
  0.0 1.6 %copy.8.expert_ids = s32[512,8]{1,0:T(8,128)} copy(s32[512,8]{0,1:T(8,128)} %param.8) | data formatting | bytes 32768 | tf_op args[1]
  1.6 1.5 %copy.9.gates = f32[512,8]{1,0:T(8,128)} copy(f32[512,8]{0,1:T(8,128)} %param.9) | data formatting | bytes 32768 | tf_op args[2]
  3.1 103.0 %shard_map.73 = bf16[512,256]{1,0:T(8,128)(2,1)} custom-call(bf16[512,256]{1,0:T(8,128)(2,1)} %tokens.1, s32[512,8]{1,0:T(8,128)} %copy.8.expert_ids, f32[512,8]{1,0:T(8,128)} %copy.9.gates, bf16[2,4096,128]{2,1,0:T(8,128)(2,1)} %query_weight.1, bf16[256,128]{1,0:T(8,128)(2,1)} %key_weight.1, bf16[256,128]{1,0:T(8,128)(2,1)} %value_weight.1, ...), custom_call_target="tpu_custom_call" | custom-call | tf_op jit(solution)/shard_map/pallas_call | solution.py:492
  106.1 1.7 %copy.11 = bf16[512,256]{1,0:T(8,128)(2,1)} copy(bf16[512,256]{1,0:T(8,128)(2,1)} %shard_map.73) | data formatting | bytes 524288

commit v2 on v1

v2 whole, which is shorter than its diff:
```python
import functools
import math

import jax
import jax.numpy as jnp
from jax import lax
from jax.experimental import pallas as pl
from jax.experimental.pallas import tpu as pltpu
from jax.sharding import PartitionSpec as P

MESH = pl.DeviceIdType.MESH
RING = 4
PEERS = RING * RING
LANES = 256
LOWEST = -1e30


def nt_dot(a, b):
    return lax.dot_general(a, b, (((1,), (1,)), ((), ())), preferred_element_type=jnp.float32)


def tn_dot(a, b):
    return lax.dot_general(a, b, (((0,), (0,)), ((), ())), preferred_element_type=jnp.float32)


def dot(a, b):
    return jnp.dot(a, b, preferred_element_type=jnp.float32)


def drain(ref, sem):
    pltpu.make_async_copy(ref, ref, sem).wait()


class PlaneGather:
    STEPS = {3: 1, 1: 3, 2: 2}

    def __init__(self, buf, rows, send_sem, recv_sem, place):
        self.buf, self.rows = buf, rows // 2
        self.send_sem, self.recv_sem, self.place = send_sem, recv_sem, place
        self.started = []

    @staticmethod
    def slot(half, first, second):
        return second * RING + first if half == 0 else first * RING + second

    @staticmethod
    def order():
        slot = PlaneGather.slot
        pieces = [(half, slot(half, first, 0)) for first in (0, 3, 1, 2) for half in range(2)]
        pieces += [
            (half, slot(half, first, second)) for first in (0, 3, 1, 2) for second in (3, 1, 2) for half in range(2)
        ]
        return pieces

    def message(self, half, phase, other, where):
        number = half * PEERS + (where * RING if phase == 0 else other * RING + where)
        rows = pl.ds(half * self.rows, self.rows)
        if phase == 0:
            src, dst = self.slot(half, 0, 0), self.slot(half, where, 0)
        else:
            src, dst = self.slot(half, other, 0), self.slot(half, other, where)
        step = self.STEPS[where]
        along_x = (half == 0) == (phase == 0)
        return pltpu.make_async_remote_copy(
            src_ref=self.buf.at[src, rows],
            dst_ref=self.buf.at[dst, rows],
            send_sem=self.send_sem.at[number],
            recv_sem=self.recv_sem.at[number],
            device_id=self.place(0, step) if along_x else self.place(step, 0),
            device_id_type=MESH,
        )

    def start(self, *key):
        copy = self.message(*key)
        copy.start()
        self.started.append(copy)

    def wait(self, *key):
        self.message(*key).wait_recv()

    def finish(self):
        for copy in self.started:
            copy.wait_send()

    def run(self, arrived, beside):
        for where in (3, 1, 2):
            for half in range(2):
                self.start(half, 0, 0, where)
        for where in (3, 1, 2):
            for half in range(2):
                self.start(half, 1, 0, where)
        beside(0)
        for half in range(2):
            arrived(half, 0)
        for first in (3, 1, 2):
            for half in range(2):
                self.wait(half, 0, 0, first)
                for where in (3, 1, 2):
                    self.start(half, 1, first, where)
        for first in (3, 1, 2):
            for half in range(2):
                arrived(half, self.slot(half, first, 0))
        for first in (0, 3, 1, 2):
            for where in (3, 1, 2):
                for half in range(2):
                    self.wait(half, 1, first, where)
                    arrived(half, self.slot(half, first, where))
            beside({0: 1, 3: 2, 1: 3, 2: 4}[first])


def layer(
    capacity,
    depth,
    tokens,
    expert_ids,
    gates,
    query_weight,
    key_weight,
    value_weight,
    output_weight,
    out,
    tok,
    qw,
    kv_part,
    kv_in,
    kv,
    q_dense,
    q_part,
    q_all,
    slot_of,
    gate_of,
    slot_row,
    spread,
    pick,
    where_row,
    wout,
    top_score,
    num,
    part_out,
    part_lse,
    heads,
    produced,
    total,
    head_send,
    head_recv,
    send_sem,
    recv_sem,
    local,
):
    ctx, exp = lax.axis_index("ctx"), lax.axis_index("exp")
    y, x = exp // RING, exp % RING
    z, core = ctx // 2, ctx % 2
    m, r = z // RING, z % RING
    other_core = 1 - core
    t, f = tokens.shape
    routes = expert_ids.shape[0]
    mine = query_weight.shape[0]
    hd = query_weight.shape[2]
    share = t // PEERS
    wide = RING * f

    def place(dy, dx):
        return (ctx, ((y + dy) % RING) * RING + (x + dx) % RING)

    def deep(dz):
        return (((z + dz) % depth) * 2 + core, exp)

    sibling = (ctx + 1 - 2 * core, exp)
    used = []

    def send(src, dst, device, number=None):
        if number is None:
            number = len(used)
            used.append(number)
        return pltpu.make_async_remote_copy(
            src_ref=src,
            dst_ref=dst,
            send_sem=send_sem.at[number],
            recv_sem=recv_sem.at[number],
            device_id=device,
            device_id_type=MESH,
        )

    def number_of():
        used.append(len(used))
        return used[-1]

    barrier = pltpu.get_barrier_semaphore()
    far_z = (1, depth - 1, 2, depth - 2, RING, depth - RING, 2 * RING)
    for dz in far_z:
        pl.semaphore_signal(barrier, inc=1, device_id=deep(dz), device_id_type=MESH)

    @pl.loop(1, PEERS)
    def _(i):
        pl.semaphore_signal(barrier, inc=1, device_id=(ctx, (exp + i) % PEERS), device_id_type=MESH)

    pl.semaphore_signal(barrier, inc=1, device_id=sibling, device_id_type=MESH)

    def row_features(yy):
        return pl.ds(pl.multiple_of(yy * wide, wide), wide)

    def features(j):
        return pl.ds(pl.multiple_of(j * f, f), f)

    quarter = hd // RING
    load_qw = pltpu.make_async_copy(query_weight.at[:, row_features(y)], qw.at[0], local.at[0])
    load_qw.start()

    def own_quarter():
        return output_weight.at[core, pl.ds(pl.multiple_of(r * quarter, quarter), quarter)]

    load_wout = pltpu.make_async_copy(own_quarter().at[:, features(exp)], wout.at[0, core, r], local.at[1])
    load_wout.start()

    tok[0] = tokens[...]
    kv_part[:, :hd] = dot(tokens[...], key_weight[...]).astype(jnp.bfloat16)
    kv_part[:, hd:] = dot(tokens[...], value_weight[...]).astype(jnp.bfloat16)

    column = lax.broadcasted_iota(jnp.int32, (128, t), 0)
    at = column // mine
    expert = ((((y + at // RING) % RING) * RING) + (x + at % RING) % RING) * mine + column % mine
    routed = jnp.zeros((128, t), jnp.float32)
    gate_sum = jnp.zeros((128, t), jnp.float32)
    for route in range(routes):
        hit = expert_ids[route : route + 1, :] == expert
        routed = jnp.where(hit, 1.0, routed)
        gate_sum = jnp.where(hit, gates[route : route + 1, :], gate_sum)
    earlier = jnp.where(
        lax.broadcasted_iota(jnp.int32, (t, t), 0) < lax.broadcasted_iota(jnp.int32, (t, t), 1), 1.0, 0.0
    ).astype(jnp.bfloat16)
    slot_row[...] = jnp.where(routed > 0.5, dot(routed.astype(jnp.bfloat16), earlier), -1.0)
    slot_of[...] = jnp.transpose(slot_row[...])
    gate_of[...] = jnp.transpose(gate_sum)

    pl.semaphore_wait(barrier, PEERS - 1 + len(far_z) + 1)

    kv_first = number_of()

    @pl.loop(1, PEERS)
    def _(i):
        j = (exp + i) % PEERS
        rows = pl.ds(pl.multiple_of(j * share, share), share)
        send(kv_part.at[rows], kv_in.at[i], (ctx, j), kv_first).start()

    qw_moves = {
        dy: send(
            query_weight.at[core, row_features((y + dy) % RING)], qw.at[RING - dy, core], place(dy, 0)
        )
        for dy in (1, 3, 2)
    }
    half = t // 2
    tok_moves = {
        3: send(tok.at[0], tok.at[3], place(0, 1)),
        1: send(tok.at[0], tok.at[1], place(0, 3)),
        "2a": send(tok.at[3, pl.ds(0, half)], tok.at[2, pl.ds(0, half)], place(0, 1)),
        "2b": send(tok.at[1, pl.ds(half, half)], tok.at[2, pl.ds(half, half)], place(0, 3)),
    }
    for move in (qw_moves[2], tok_moves[1], tok_moves[3], qw_moves[1], qw_moves[3]):
        move.start()

    w_first = number_of()

    def send_wout():
        @pl.loop(1, PEERS)
        def _(i):
            dy, dx = i // RING, i % RING
            j = ((y + dy) % RING) * RING + (x + dx) % RING
            back = ((RING - dy) % RING) * RING + (RING - dx) % RING
            send(own_quarter().at[:, features(j)], wout.at[back, core, r], (ctx, j), w_first).start()

    send_wout()

    drain(kv_in.at[pl.ds(1, PEERS - 1)], recv_sem.at[kv_first])
    summed = kv_part[pl.ds(pl.multiple_of(exp * share, share), share)].astype(jnp.float32)
    for i in range(1, PEERS):
        summed += kv_in[i].astype(jnp.float32)
    kv[m, r, core, x] = summed.astype(jnp.bfloat16)
    stride_moves = [
        send(kv.at[m, r, core, x], kv.at[m, r, core, x], deep(dz)) for dz in (2 * RING, RING, 3 * RING)
    ]
    for move in stride_moves:
        move.start()
    m4, m8, m12 = (m + 1) % RING, (m + 2) % RING, (m + 3) % RING

    def got(piece, move_number):
        return send(piece, piece, sibling, move_number)

    first_of_stride = used[-3]
    stride_in = [
        got(kv.at[mm, r, core, x], first_of_stride + n) for n, mm in enumerate((m8, m12, m4))
    ]

    r1, r2, r3 = (r + 1) % RING, (r + 2) % RING, (r + 3) % RING
    low_m, high_m = pl.ds(0, RING // 2), pl.ds(RING // 2, RING // 2)
    residue_moves = [
        send(kv.at[low_m, r, core, x], kv.at[low_m, r, core, x], deep(2)),
        send(kv.at[high_m, r, core, x], kv.at[high_m, r, core, x], deep(depth - 2)),
        send(kv.at[:, r, core, x], kv.at[:, r, core, x], deep(1)),
        send(kv.at[:, r, core, x], kv.at[:, r, core, x], deep(depth - 1)),
    ]
    first_of_residue = used[-4]
    residue_in = [
        got(kv.at[low_m, r2, core, x], first_of_residue),
        got(kv.at[high_m, r2, core, x], first_of_residue + 1),
        got(kv.at[:, r3, core, x], first_of_residue + 2),
        got(kv.at[:, r1, core, x], first_of_residue + 3),
    ]
    x1, x2, x3 = (x + 1) % RING, (x + 2) % RING, (x + 3) % RING
    x_numbers = {step: number_of() for step in (1, 3, 2)}
    x_moves = []

    def push_along_x(rr):
        for step in (1, 3, 2):
            piece = kv.at[:, rr, core, x]
            x_moves.append(send(piece, piece, place(0, step), x_numbers[step]))
            x_moves[-1].start()

    columns = (x, x3, x1, x2)
    across = [send(kv.at[:, :, core, xx], kv.at[:, :, core, xx], sibling) for xx in columns]
    first_across = used[-4]
    across_in = [got(kv.at[:, :, other_core, xx], first_across + n) for n, xx in enumerate(columns)]

    position = lax.broadcasted_iota(jnp.int32, (t, 128), 0)
    high = (position // 16).astype(jnp.float32).astype(jnp.bfloat16)
    low = (position % 16).astype(jnp.float32).astype(jnp.bfloat16)
    place_of = jnp.concatenate([high, low], axis=1)
    slots = lax.broadcasted_iota(jnp.int32, (capacity, t), 0).astype(jnp.float32)
    for n in range(RING * mine):
        line = (n // mine) * (RING * mine) + n % mine
        pick[n] = jnp.where(slot_row[line : line + 1, :] == slots, 1.0, 0.0).astype(jnp.bfloat16)
        found = dot(pick[n], place_of)
        where_row[n] = 16.0 * found[:, :128] + found[:, 128:]

    tok_moves[3].wait_recv()
    tok_moves["2a"].start()
    tok_moves[1].wait_recv()
    tok_moves["2b"].start()

    for move in stride_in:
        move.wait_recv()
    for move in residue_moves:
        move.start()
    push_along_x(r)

    pieces = PlaneGather.order()

    def fill_spread(begin, end):
        lanes = lax.broadcasted_iota(jnp.int32, (t, LANES), 1).astype(jnp.float32)
        for p in range(begin, end):
            part, slot = pieces[p]
            n = slot * mine + part
            spread[:, p * LANES : (p + 1) * LANES] = jnp.where(
                slot_of[:, n : n + 1] == lanes, gate_of[:, n : n + 1], 0.0
            ).astype(jnp.bfloat16)

    fill_spread(0, 8)
    residue_in[2].wait_recv()
    push_along_x(r3)
    residue_in[3].wait_recv()
    push_along_x(r1)
    residue_in[0].wait_recv()
    residue_in[1].wait_recv()
    push_along_x(r2)
    across[0].start()
    fill_spread(8, 12)
    load_wout.wait()
    drain(wout.at[pl.ds(1, PEERS - 1), core, r], recv_sem.at[w_first])
    low_s, high_s = pl.ds(0, PEERS // 2), pl.ds(PEERS // 2, PEERS // 2)
    w_moves = [
        send(wout.at[low_s, core, r], wout.at[low_s, core, r], deep(2)),
        send(wout.at[high_s, core, r], wout.at[high_s, core, r], deep(depth - 2)),
        send(wout.at[:, core, r], wout.at[:, core, r], deep(1)),
        send(wout.at[:, core, r], wout.at[:, core, r], deep(depth - 1)),
    ]
    first_of_w = used[-4]
    w_in = [
        got(wout.at[low_s, core, r2], first_of_w),
        got(wout.at[high_s, core, r2], first_of_w + 1),
        got(wout.at[:, core, r3], first_of_w + 2),
        got(wout.at[:, core, r1], first_of_w + 3),
    ]
    for move in w_moves:
        move.start()

    fill_spread(12, 16)


    qw_across, qw_across_in = {}, {}
    for dy in (1, 3, 2):
        slot = RING - dy
        qw_moves[dy].wait_recv()
        qw_across[slot] = send(qw.at[slot, core], qw.at[slot, core], sibling)
        qw_across_in[slot] = got(qw.at[slot, other_core], used[-1])
        qw_across[slot].start()

    tok_moves["2a"].wait_recv()
    tok_moves["2b"].wait_recv()

    def partial_queries(dy):
        for part in range(2):
            rows = pl.ds(part * half, half)
            acc = jnp.zeros((half, mine * hd), jnp.float32)
            for dx in range(RING):
                own = features((x + dx) % RING)
                weight = jnp.concatenate([qw[dy, a, own] for a in range(mine)], axis=1)
                acc += dot(tok[dx, rows], weight)
            q_dense[rows] = acc.astype(jnp.bfloat16)
        for a in range(mine):
            q_part[dy, pl.ds(a * capacity, capacity)] = dot(
                pick[dy * mine + a], q_dense[:, a * hd : (a + 1) * hd]
            ).astype(jnp.bfloat16)

    q_part_moves = {
        dy: send(q_part.at[dy], q_part.at[2 * RING - dy], place(dy, 0)) for dy in range(1, RING)
    }
    load_qw.wait()
    for dy in (3, 1, 2):
        qw_across_in[dy].wait_recv()
        partial_queries(dy)
        q_part_moves[dy].start()
    partial_queries(0)

    fill_spread(16, 2 * PEERS)
    for n, step in enumerate((1, 3, 2)):
        drain(kv.at[:, :, core, columns[n + 1]], recv_sem.at[x_numbers[step]])
        across[n + 1].start()

    for dy in (3, 1, 2):
        q_part_moves[dy].wait_recv()
    q_all[0] = functools.reduce(
        jnp.add, [q_part[s].astype(jnp.float32) for s in (0, 5, 6, 7)]
    ).astype(jnp.bfloat16)
    q_moves = {dy: send(q_all.at[0], q_all.at[RING - dy], place(dy, 0)) for dy in range(1, RING)}
    for dy in (2, 1, 3):
        q_moves[dy].start()

    for move in across_in:
        move.wait_recv()

    factor = math.log2(math.e) / math.sqrt(hd)
    groups = z // 4
    span = RING * share
    block = 8 * span

    def attend(dy):
        top_score[...] = jnp.full_like(top_score, LOWEST)
        num[...] = jnp.zeros_like(num)

        def step(g, masked):
            keys = kv[g].reshape(block, 2 * hd)
            values = jnp.concatenate([keys[:, hd:], jnp.ones((block, hd), jnp.bfloat16)], axis=1)
            keys = keys[:, :hd]
            for a in range(mine):
                rows = pl.ds(a * capacity, capacity)
                scores = nt_dot(q_all[dy, rows], keys)
                if masked:
                    index = lax.broadcasted_iota(jnp.int32, (1, block), 1)
                    at = (8 * g + index // span - ctx) * t + y * span + index % span
                    scores = jnp.where(
                        at.astype(jnp.float32) <= where_row[dy * mine + a][:, 0:1], scores, LOWEST
                    )
                before = top_score[rows, 0:1]
                now = jnp.maximum(before, jnp.max(scores, axis=1, keepdims=True))
                weights = jnp.exp2((scores - now) * factor).astype(jnp.bfloat16)
                num[rows] = num[rows] * jnp.exp2((before - now) * factor) + dot(weights, values)
                top_score[rows] = jnp.broadcast_to(now, (capacity, 128))

        @pl.loop(0, groups)
        def _(g):
            step(g, False)

        step(groups, True)
        for a in range(mine):
            rows = pl.ds(a * capacity, capacity)
            norm = num[rows, hd:]
            part_out[dy, rows] = (num[rows, :hd] / norm).astype(jnp.bfloat16)
            lse = top_score[rows, 0:1] * factor + jnp.log2(norm[:, 0:1])
            part_lse[dy, pl.ds(a * 8, 8)] = to_row(lse)

    def diagonal():
        return lax.broadcasted_iota(jnp.int32, (capacity, LANES), 0) == lax.broadcasted_iota(
            jnp.int32, (capacity, LANES), 1
        )

    def to_row(values):
        row = jnp.sum(jnp.where(diagonal(), values, 0.0), axis=0, keepdims=True)
        return jnp.broadcast_to(row, (8, LANES))

    def to_column(row):
        return jnp.sum(jnp.where(diagonal(), row, 0.0), axis=1, keepdims=True)

    moves = []
    for dy in (0, 1, 3, 2):
        if dy:
            q_moves[RING - dy].wait_recv()
        attend(dy)
        if dy:
            moves.append(send(part_out.at[dy], part_out.at[2 * RING - dy], place(dy, 0)))
            moves.append(send(part_lse.at[dy], part_lse.at[2 * RING - dy], place(dy, 0)))
            moves[-2].start()
            moves[-1].start()
        if dy == 0:
            for move in w_in:
                move.wait_recv()
            w_across = send(wout.at[:, core], wout.at[:, core], sibling)
            w_across_in = got(wout.at[:, other_core], used[-1])
            w_across.start()

    produced[...] = jnp.zeros_like(produced)
    for move in moves:
        move.wait_recv()
    for a in range(mine):
        rows = pl.ds(a * capacity, capacity)
        parts = (0, 5, 6, 7)
        lses = [to_column(part_lse[s, pl.ds(a * 8, 1)]) for s in parts]
        top = functools.reduce(jnp.maximum, lses)
        weights = [jnp.exp2(lse - top) for lse in lses]
        norm = functools.reduce(jnp.add, weights)
        rows_sum = functools.reduce(
            jnp.add, [w * part_out[s, rows].astype(jnp.float32) for w, s in zip(weights, parts)]
        )
        heads[0, rows] = (rows_sum / norm).astype(jnp.bfloat16)

    seen = []

    def make_output(part, slot):
        begin = len(seen) * LANES
        seen.append((part, slot))
        made = dot(heads[slot, pl.ds(part * capacity, capacity)], wout[slot, part].reshape(hd, f))
        produced[begin : begin + capacity] = made.astype(jnp.bfloat16)

    added = [0]

    def beside(stage):
        if stage == 0:
            w_across_in.wait_recv()
        else:
            begin, end = added[0] * LANES, len(seen) * LANES
            part = dot(spread[:, begin:end], produced[begin:end])
            if stage == 1:
                total[...] = part
            elif stage < 4:
                total[...] += part
            else:
                out[...] = (total[...] + part).astype(jnp.bfloat16)
            added[0] = len(seen)

    head_gather = PlaneGather(heads, mine * capacity, head_send, head_recv, place)
    head_gather.run(make_output, beside)
    assert seen == pieces

    for step in (1, 3, 2):
        drain(kv.at[:, :, core, x], send_sem.at[x_numbers[step]])
    head_gather.finish()
    drain(kv_in.at[pl.ds(1, PEERS - 1)], send_sem.at[kv_first])
    drain(wout.at[pl.ds(1, PEERS - 1), core, r], send_sem.at[w_first])
    for copy in (
        *qw_moves.values(),
        *tok_moves.values(),
        *stride_moves,
        *residue_moves,
        *across,
        *w_moves,
        *qw_across.values(),
        *q_part_moves.values(),
        *q_moves.values(),
        *moves,
        w_across,
    ):
        copy.wait_send()


def per_device(depth, tokens, expert_ids, gates, query_weight, key_weight, value_weight, output_weight):
    t, f = tokens.shape
    routes = expert_ids.shape[1]
    mine, model, hd = query_weight.shape
    experts = mine * PEERS
    capacity = min(t, max(2, 5 * t * routes // (4 * experts)))
    owned = mine * capacity
    share = t // PEERS
    bf16, f32 = jnp.bfloat16, jnp.float32
    vmem, anywhere = pl.BlockSpec(memory_space=pltpu.VMEM), pl.BlockSpec(memory_space=pl.ANY)
    return pl.pallas_call(
        functools.partial(layer, capacity, depth),
        out_shape=jax.ShapeDtypeStruct((t, f), bf16),
        in_specs=[vmem, vmem, vmem, anywhere, vmem, vmem, anywhere],
        out_specs=vmem,
        scratch_shapes=[
            pltpu.VMEM((RING, t, f), bf16),
            pltpu.VMEM((RING, mine, RING * f, hd), bf16),
            pltpu.VMEM((t, 2 * hd), bf16),
            pltpu.VMEM((PEERS, share, 2 * hd), bf16),
            pltpu.VMEM((depth // RING, RING, 2, RING, share, 2 * hd), bf16),
            pltpu.VMEM((t, mine * hd), bf16),
            pltpu.VMEM((2 * RING, owned, hd), bf16),
            pltpu.VMEM((RING, owned, hd), bf16),
            pltpu.VMEM((t, 128), f32),
            pltpu.VMEM((t, 128), f32),
            pltpu.VMEM((128, t), f32),
            pltpu.VMEM((t, experts * LANES), bf16),
            pltpu.VMEM((RING * mine, capacity, t), bf16),
            pltpu.VMEM((RING * mine, capacity, 128), f32),
            pltpu.VMEM((PEERS, mine, RING, hd // RING, f), bf16),
            pltpu.VMEM((owned, 128), f32),
            pltpu.VMEM((owned, 2 * hd), f32),
            pltpu.VMEM((2 * RING, owned, hd), bf16),
            pltpu.VMEM((2 * RING, 8 * mine, LANES), f32),
            pltpu.VMEM((PEERS, owned, hd), bf16),
            pltpu.VMEM((experts * LANES, f), bf16),
            pltpu.VMEM((t, f), f32),
            pltpu.SemaphoreType.DMA((40,)),
            pltpu.SemaphoreType.DMA((40,)),
            pltpu.SemaphoreType.DMA((64,)),
            pltpu.SemaphoreType.DMA((64,)),
            pltpu.SemaphoreType.DMA((2,)),
        ],
        compiler_params=pltpu.CompilerParams(
            collective_id=0, has_side_effects=True, vmem_limit_bytes=56 * 1024 * 1024
        ),
    )(tokens, expert_ids.T, gates.T, query_weight, key_weight, value_weight, output_weight)


def solution(mesh):
    in_specs = (
        P("ctx", "exp"),
        P("ctx", None),
        P("ctx", None),
        P("exp", None, None),
        P("exp", None),
        P("exp", None),
        P("exp", None, None),
    )
    out_specs = P("ctx", "exp")
    return jax.shard_map(
        functools.partial(per_device, mesh.shape["ctx"] // 2),
        mesh=mesh,
        in_specs=in_specs,
        out_specs=out_specs,
        check_vma=False,
    )
```

time: 108 us -> 83.9 us (0.78)
  the two profiles are of different devices: /device:TPU:489 before, /device:TPU:1 now
where the time goes in v2:
time: 83.9 us; the launch traced here: 82.8 us
  Pallas kernels  81.1 us (97%)
  local copies, waits for them, and re-layouts  1.67 us (2%)
    pallas_call x1, Pallas kernels, per_device(): pl.pallas_call(functools.partial(layer, capacity, depth), out_shape=jax.S...  81.1 us

profile of v2, /device:TPU:1, one launch (start us, length us, event | category | flops | bytes accessed | tf_op | source)
XLA Modules:
  0.0 82.8 jit_solution(7232776770257832045)
XLA Ops:
  0.0 81.1 %shard_map.73 = bf16[512,256]{1,0:T(8,128)(2,1)} custom-call(bf16[512,256]{1,0:T(8,128)(2,1)} %tokens.1, s32[8,512]{1,0:T(8,128)} %bitcast.2, f32[8,512]{1,0:T(8,128)} %bitcast.3, bf16[2,4096,128]{2,1,0:T(8,128)(2,1)} %query_weight.1, bf16[256,128]{1,0:T(8,128)(2,1)} %key_weight.1, bf16[256,128]{1,0:T(8,128)(2,1)} %value_weight.1, ...), custom_call_target="tpu_custom_call" | custom-call | tf_op jit(solution)/shard_map/pallas_call | solution.py:583
  81.1 1.7 %copy.9 = bf16[512,256]{1,0:T(8,128)(2,1)} copy(bf16[512,256]{1,0:T(8,128)(2,1)} %shard_map.73) | data formatting | bytes 524288

commit v3 on v2

--- a/solution.py
+++ b/solution.py
@@ -246,8 +246,11 @@
         dy: send(
             query_weight.at[core, row_features((y + dy) % RING)], qw.at[RING - dy, core], place(dy, 0)
         )
-        for dy in (1, 3, 2)
+        for dy in (1, 3)
     }
+    part = pl.ds(pl.multiple_of(r * f, f), f)
+    far_quarter = pl.ds(pl.multiple_of(((y + 2) % RING) * wide + r * f, f), f)
+    qw_moves[2] = send(query_weight.at[core, far_quarter], qw.at[2, core, part], place(2, 0))
     half = t // 2
     tok_moves = {
         3: send(tok.at[0], tok.at[3], place(0, 1)),
@@ -291,6 +294,32 @@
     ]
 
     r1, r2, r3 = (r + 1) % RING, (r + 2) % RING, (r + 3) % RING
+
+    def far_part(rr, begin, rows):
+        return qw.at[2, core, pl.ds(pl.multiple_of(rr * f + begin, f // 2), rows)]
+
+    far_moves = [
+        send(far_part(r, 0, f // 2), far_part(r, 0, f // 2), deep(2)),
+        send(far_part(r, f // 2, f // 2), far_part(r, f // 2, f // 2), deep(depth - 2)),
+        send(far_part(r, 0, f), far_part(r, 0, f), deep(1)),
+        send(far_part(r, 0, f), far_part(r, 0, f), deep(depth - 1)),
+    ]
+    first_of_far = used[-4]
+    far_in = [
+        got(far_part(r2, 0, f // 2), first_of_far),
+        got(far_part(r2, f // 2, f // 2), first_of_far + 1),
+        got(far_part(r3, 0, f), first_of_far + 2),
+        got(far_part(r1, 0, f), first_of_far + 3),
+    ]
+    qw_moves[2].wait_recv()
+    for move in far_moves:
+        move.start()
+
+    tok_moves[3].wait_recv()
+    tok_moves["2a"].start()
+    tok_moves[1].wait_recv()
+    tok_moves["2b"].start()
+
     low_m, high_m = pl.ds(0, RING // 2), pl.ds(RING // 2, RING // 2)
     residue_moves = [
         send(kv.at[low_m, r, core, x], kv.at[low_m, r, core, x], deep(2)),
@@ -330,11 +359,6 @@
         pick[n] = jnp.where(slot_row[line : line + 1, :] == slots, 1.0, 0.0).astype(jnp.bfloat16)
         found = dot(pick[n], place_of)
         where_row[n] = 16.0 * found[:, :128] + found[:, 128:]
-
-    tok_moves[3].wait_recv()
-    tok_moves["2a"].start()
-    tok_moves[1].wait_recv()
-    tok_moves["2b"].start()
 
     for move in stride_in:
         move.wait_recv()
@@ -388,7 +412,8 @@
     qw_across, qw_across_in = {}, {}
     for dy in (1, 3, 2):
         slot = RING - dy
-        qw_moves[dy].wait_recv()
+        for move in far_in if dy == 2 else [qw_moves[dy]]:
+            move.wait_recv()
         qw_across[slot] = send(qw.at[slot, core], qw.at[slot, core], sibling)
         qw_across_in[slot] = got(qw.at[slot, other_core], used[-1])
         qw_across[slot].start()
@@ -413,11 +438,11 @@
     q_part_moves = {
         dy: send(q_part.at[dy], q_part.at[2 * RING - dy], place(dy, 0)) for dy in range(1, RING)
     }
-    load_qw.wait()
     for dy in (3, 1, 2):
         qw_across_in[dy].wait_recv()
         partial_queries(dy)
         q_part_moves[dy].start()
+    load_qw.wait()
     partial_queries(0)
 
     fill_spread(16, 2 * PEERS)
@@ -556,6 +581,7 @@
     drain(wout.at[pl.ds(1, PEERS - 1), core, r], send_sem.at[w_first])
     for copy in (
         *qw_moves.values(),
+        *far_moves,
         *tok_moves.values(),
         *stride_moves,
         *residue_moves,

time: 83.9 us -> 81.2 us (0.968)
  Pallas kernels: 81.1 us -> 78.3 us
    pallas_call x1, Pallas kernels: 81.1 us -> 78.3 us  [per_device(): pl.pallas_call(functools.partial(layer, capacity, depth), out_shape=jax.S...]
where the time goes in v3:
time: 81.2 us; the launch traced here: 80 us
  Pallas kernels  78.3 us (96%)
  local copies, waits for them, and re-layouts  1.67 us (2%)
    pallas_call x1, Pallas kernels, per_device(): pl.pallas_call(functools.partial(layer, capacity, depth), out_shape=jax.S...  78.3 us
    unnamed x1, local copies, waits for them, and re-layouts  1.67 us

profile of v3, /device:TPU:1, one launch (start us, length us, event | category | flops | bytes accessed | tf_op | source)
XLA Modules:
  0.0 80.0 jit_solution(10735853422591612369)
XLA Ops:
  0.0 78.3 %shard_map.73 = bf16[512,256]{1,0:T(8,128)(2,1)} custom-call(bf16[512,256]{1,0:T(8,128)(2,1)} %tokens.1, s32[8,512]{1,0:T(8,128)} %bitcast.2, f32[8,512]{1,0:T(8,128)} %bitcast.3, bf16[2,4096,128]{2,1,0:T(8,128)(2,1)} %query_weight.1, bf16[256,128]{1,0:T(8,128)(2,1)} %key_weight.1, bf16[256,128]{1,0:T(8,128)(2,1)} %value_weight.1, ...), custom_call_target="tpu_custom_call" | custom-call | tf_op jit(solution)/shard_map/pallas_call | solution.py:609
  78.3 1.7 %copy.9 = bf16[512,256]{1,0:T(8,128)(2,1)} copy(bf16[512,256]{1,0:T(8,128)(2,1)} %shard_map.73) | data formatting | bytes 524288

commit v4 on v3

--- a/solution.py
+++ b/solution.py
@@ -83,7 +83,7 @@
             copy.wait_send()
 
     def run(self, arrived, beside):
-        for where in (3, 1, 2):
+        for where in (2, 3, 1):
             for half in range(2):
                 self.start(half, 0, 0, where)
         for where in (3, 1, 2):
@@ -95,7 +95,7 @@
         for first in (3, 1, 2):
             for half in range(2):
                 self.wait(half, 0, 0, first)
-                for where in (3, 1, 2):
+                for where in (2, 3, 1):
                     self.start(half, 1, first, where)
         for first in (3, 1, 2):
             for half in range(2):
@@ -446,10 +446,6 @@
     partial_queries(0)
 
     fill_spread(16, 2 * PEERS)
-    for n, step in enumerate((1, 3, 2)):
-        drain(kv.at[:, :, core, columns[n + 1]], recv_sem.at[x_numbers[step]])
-        across[n + 1].start()
-
     for dy in (3, 1, 2):
         q_part_moves[dy].wait_recv()
     q_all[0] = functools.reduce(
@@ -459,6 +455,9 @@
     for dy in (2, 1, 3):
         q_moves[dy].start()
 
+    for n, step in enumerate((1, 3, 2)):
+        drain(kv.at[:, :, core, columns[n + 1]], recv_sem.at[x_numbers[step]])
+        across[n + 1].start()
     for move in across_in:
         move.wait_recv()
 
@@ -515,7 +514,7 @@
         return jnp.sum(jnp.where(diagonal(), row, 0.0), axis=1, keepdims=True)
 
     moves = []
-    for dy in (0, 1, 3, 2):
+    for dy in (0, 1, 2, 3):
         if dy:
             q_moves[RING - dy].wait_recv()
         attend(dy)

time: 81.2 us -> 80.7 us (level)
  no operation moved by 1% of the time
where the time goes in v4:
time: 80.7 us; the launch traced here: 79.5 us
  Pallas kernels  77.8 us (96%)
  local copies, waits for them, and re-layouts  1.67 us (2%)
    pallas_call x1, Pallas kernels, per_device(): pl.pallas_call(functools.partial(layer, capacity, depth), out_shape=jax.S...  77.8 us
    unnamed x1, local copies, waits for them, and re-layouts  1.67 us

profile of v4, /device:TPU:1, one launch (start us, length us, event | category | flops | bytes accessed | tf_op | source)
XLA Modules:
  0.0 79.5 jit_solution(2772798858442897649)
XLA Ops:
  0.0 77.8 %shard_map.73 = bf16[512,256]{1,0:T(8,128)(2,1)} custom-call(bf16[512,256]{1,0:T(8,128)(2,1)} %tokens.1, s32[8,512]{1,0:T(8,128)} %bitcast.2, f32[8,512]{1,0:T(8,128)} %bitcast.3, bf16[2,4096,128]{2,1,0:T(8,128)(2,1)} %query_weight.1, bf16[256,128]{1,0:T(8,128)(2,1)} %key_weight.1, bf16[256,128]{1,0:T(8,128)(2,1)} %value_weight.1, ...), custom_call_target="tpu_custom_call" | custom-call | tf_op jit(solution)/shard_map/pallas_call | solution.py:608
  77.8 1.7 %copy.9 = bf16[512,256]{1,0:T(8,128)(2,1)} copy(bf16[512,256]{1,0:T(8,128)(2,1)} %shard_map.73) | data formatting | bytes 524288
